TPU v7x, 32 devices: a whole 2x2x4 slice. The times are simulated.
32 devices in a mesh: src: 4 (over z), tm: 8 (over y, x, core).
Axes of the slice: x: 2, y: 2, z: 4, core: 2. Of those that a mesh axis runs over, the one named last changes fastest.
Arguments:
- src_design: float32 [4096, 5, 128], P(('src', 'tm')), may hold values from -6 to 6
- att_design: float32 [4096, 3, 128], P(('src', 'tm')), may hold values from -6 to 6
- obs_frac: float32 [4096, 128], P(('src', 'tm')), may hold values from 0 to 1
- obs_knot: int32 [4096, 128], P(('src', 'tm')), may hold values from 0 to 124
- observed: float32 [4096, 128], P(('src', 'tm'))
- tile_slot: int32 [4096], P(('src', 'tm')), may hold values from 0 to 63, as said below
- tile_offset: int32 [4096], P(('src', 'tm')), may hold values from 0 to 4095
- tile_valid: int32 [4096], P(('src', 'tm')), may hold values from 8 to 128, as said below
- slot_block: int32 [256, 8], P(('src', 'tm')), may hold values from 0 to 31, as said below
Outputs:
- src_solution: float32 [1024, 5, 128], P(('src', 'tm'))
- att_solution: float32 [3, 32768], P(None, 'tm')
Inputs may be any that keep to these rules, and one draw needn't show every extreme that they name: `slot_block`: each row lists 8 distinct local source blocks. `tile_slot`: every slot of every device is named by at least one of that device's tiles. Rows at or after tile_valid are padding.
All inputs are finite; a program needn't handle non-finite values.
Results may differ from a plain program's by a relative error of at most 0.00026.
Values sent between devices are 32-bit elements; how exact they have to be, the bound alone decides.
No kernel may reach another device: no remote copies, remote signals or barrier semaphores. Data moves between devices by JAX's collectives and lax.ppermute only.
A program may use at most 64 MiB of HBM per device.

v0:
```python
import jax
import jax.numpy as jnp
from jax import lax
from jax.sharding import PartitionSpec as P

KN = 4096
HW = 128
SB_DEV = 32
ITERS = 2
damping = 1.0


def passed_along(block, axis, distance):
    devices = range(lax.axis_size(axis))
    route = [(i - distance, i) for i in devices if i - distance in devices]
    return lax.ppermute(block, axis, route)


def spline_weights(fraction):
    remain = 1.0 - fraction
    square = fraction * fraction
    cubed = square * fraction
    return (
        remain * remain * remain / 6.0,
        (3.0 * cubed - 6.0 * square + 4.0) / 6.0,
        (-3.0 * cubed + 3.0 * square + 3.0 * fraction + 1.0) / 6.0,
        cubed / 6.0,
    )


def spline_basis(knots, wstack):
    columns = lax.broadcasted_iota(jnp.int32, (1, 1, HW), 2)
    total = jnp.zeros((knots.shape[0], knots.shape[1], HW), jnp.float32)
    for order in range(4):
        hit = (knots[:, :, None] + order == columns).astype(jnp.float32)
        total = total + wstack[:, order, :][:, :, None] * hit
    return total


def shards(
    src_design,
    att_design,
    obs_frac,
    obs_knot,
    observed,
    tile_slot,
    tile_offset,
    tile_valid,
    slot_block,
):
    tile_count, params, lane_count = src_design.shape
    tm_count = lax.axis_size("tm")
    slot_cap = slot_block.shape[1]
    on_first = lax.axis_index("src") == 0
    valid_rows = (
        lax.broadcasted_iota(jnp.int32, (tile_count, lane_count), 1) < tile_valid[:, None]
    ).astype(jnp.float32)
    wstack = jnp.stack(spline_weights(obs_frac), axis=1)
    block_len = min(32, tile_count)
    block_count = tile_count // block_len
    knot_blocks = obs_knot.reshape(block_count, block_len, lane_count)
    weight_blocks = wstack.reshape(block_count, block_len, 4, lane_count)
    window_index = tile_offset[:, None] + lax.broadcasted_iota(jnp.int32, (tile_count, HW), 1)
    owner_tm = tile_slot // slot_cap
    shard_block = owner_tm * SB_DEV + slot_block.reshape(-1)[tile_slot]

    def return_sources(src_part):
        per_block = jax.ops.segment_sum(src_part, shard_block, num_segments=tm_count * SB_DEV)
        return lax.psum_scatter(per_block, "tm", scatter_dimension=0, tiled=True)

    def cut_window(extended, start):
        return lax.dynamic_slice(extended, (jnp.int32(0), start), (3, HW))

    def forward_block(items):
        knots, wts, window = items
        basis = spline_basis(knots, wts)
        return jnp.einsum("trk,tak->tar", basis, window, precision=lax.Precision.HIGHEST)

    def adjoint_block(items):
        knots, wts, scaled = items
        basis = spline_basis(knots, wts)
        return jnp.einsum("trk,tar->tak", basis, scaled, precision=lax.Precision.HIGHEST)

    def adjoint(resid):
        src_term = return_sources(src_design * resid[:, None, :])
        scaled = att_design * resid[:, None, :]
        win_sums = lax.map(
            adjoint_block,
            (knot_blocks, weight_blocks, scaled.reshape(block_count, block_len, 3, lane_count)),
        )
        win_sums = jnp.transpose(win_sums.reshape(tile_count, 3, HW), (1, 0, 2))
        knot_part = jnp.zeros((3, KN + HW), jnp.float32).at[:, window_index].add(win_sums)
        spill = passed_along(knot_part[:, KN:], "tm", 1)
        own_part = knot_part[:, :KN].at[:, :HW].add(spill)
        return (src_term, lax.psum(own_part, "src"))

    def local_dot(left, right):
        return jnp.sum(left[0] * right[0]) + jnp.where(on_first, jnp.sum(left[1] * right[1]), 0.0)

    def norm_sum(vector):
        return lax.psum(local_dot(vector, vector), ("src", "tm"))

    def combine(first, scale, second):
        return (first[0] + scale * second[0], first[1] + scale * second[1])

    solution = (
        jnp.zeros((SB_DEV, params, lane_count), jnp.float32),
        jnp.zeros((3, KN), jnp.float32),
    )
    residual = adjoint(valid_rows * observed)
    direction = residual
    norm_now = norm_sum(residual)
    for step in range(ITERS):
        dir_att = direction[1]
        whole = lax.all_gather(direction[0], "tm", axis=0, tiled=True)
        src_tiles = whole[shard_block]
        rim_knots = passed_along(dir_att[:, :HW], "tm", -1)
        forward_extended = jnp.concatenate([dir_att, rim_knots], axis=1)
        windows = jax.vmap(cut_window, in_axes=(None, 0))(forward_extended, tile_offset)
        spline = lax.map(
            forward_block,
            (knot_blocks, weight_blocks, windows.reshape(block_count, block_len, 3, HW)),
        )
        spline = spline.reshape(tile_count, 3, lane_count)
        predicted = jnp.sum(src_design * src_tiles, axis=1) + jnp.sum(att_design * spline, axis=1)
        image = adjoint(valid_rows * predicted)
        image = (image[0] + damping * direction[0], image[1] + damping * direction[1])
        curv = lax.psum(local_dot(direction, image), ("src", "tm"))
        step_len = norm_now / curv
        solution = combine(solution, step_len, direction)
        residual = combine(residual, -step_len, image)
        if step + 1 < ITERS:
            norm_next = norm_sum(residual)
            direction = combine(residual, norm_next / norm_now, direction)
            norm_now = norm_next
    return (solution[0], solution[1])


def solution(mesh):
    placed = (
        P(("src", "tm"), None, None),
        P(("src", "tm"), None, None),
        P(("src", "tm"), None),
        P(("src", "tm"), None),
        P(("src", "tm"), None),
        P(("src", "tm")),
        P(("src", "tm")),
        P(("src", "tm")),
        P(("src", "tm"), None),
    )
    return jax.shard_map(
        shards,
        mesh=mesh,
        in_specs=placed,
        out_specs=(P(("src", "tm"), None, None), P(None, "tm")),
        check_vma=False,
    )
```

profile of v0, /device:TPU:0, one launch (start us, length us, event | category | flops | bytes accessed | tf_op | source)
XLA Modules:
  0.0 1335.6 jit_solution(15962289822977489841)
XLA Ops:
  12.8 4.9 scatter_fusion
  19.2 35.6 %while.55 = (s32[]{:T(128)}, f32[4,32,3,128]{3,2,1,0:T(4,128)S(1)}, f32[4,32,3,128]{3,2,1,0:T(4,128)S(1)}, s32[4,32,128]{2,1,0:T(8,128)S(1)}, f32[4,32,4,128]{3,1,2,0:T(8,128)S(1)}, /*index=5*/s32[]{:T(128)}) while((s32[]{:T(128)}, f32[4,32,3,128]{3,2,1,0:T(4,128)S(1)}, f32[4,32,3,128]{3,2,1,0:T(4,128)S(1)}, s32[4,32,128]{2,1,0:T(8,128)S(1)}, ...), condition=%wide.region_4.5_spmd, body=%wide.region_3.4_spmd.sunk | while | flops 24653824 | bytes 623701 | solution.py:87
  19.3 8.8 fusion.179
  28.2 8.8 fusion.179
  37.1 8.8 fusion.179
  46.0 8.8 fusion.179
  54.9 4.9 copy.41
  59.7 89.1 %scatter_custom_fusion.1 = f32[3,4224]{0,1:T(8,128)} fusion(s32[16384]{0:T(1024)S(1)} %fusion.158, f32[16384,3]{1,0:T(8,128)} %bitcast.183, f32[]{:T(128)} %constant.206.clone.1), kind=kCustom, calls=%fused_computation.205 | custom fusion | flops 49152 | bytes 51200 | tf_op jit(solution)/shard_map/scatter-add | solution.py:92
  157.9 80.0 %psum.49 = f32[3,4096]{0,1:T(8,128)S(1)} all-reduce(f32[3,4096]{0,1:T(8,128)} %fusion.155), channel_id=1, replica_groups=mesh['src'=4,'tm'=8] {'src'}, use_global_device_ids=true, to_apply=%region_7.8 | all-reduce | flops 12288 | bytes 98304 | tf_op jit(solution)/shard_map/psum | solution.py:95
  241.3 185.1 %while.60 = (s32[]{:T(128)}, f32[3,4224]{1,0:T(4,128)S(1)}, s32[128,2]{0,1:T(2,128)S(1)}, f32[128,3,128]{2,1,0:T(4,128)S(1)}, s32[]{:T(128)}) while((s32[]{:T(128)}, f32[3,4224]{1,0:T(4,128)S(1)}, s32[128,2]{0,1:T(2,128)S(1)}, f32[128,3,128]{2,1,0:T(4,128)S(1)}, s32[]{:T(128)}) %tuple.181), condition=%wide.while_cond.3, body=%wide.while_body.3.sunk | while | flops 2 | bytes 4201 | solution.py:72
  426.4 41.1 %while.56 = (s32[]{:T(128)}, f32[4,32,3,128]{3,2,1,0:T(4,128)S(1)}, f32[4,32,3,128]{3,2,1,0:T(4,128)S(1)}, s32[4,32,128]{2,1,0:T(8,128)S(1)}, f32[4,32,4,128]{3,1,2,0:T(8,128)S(1)}, /*index=5*/s32[]{:T(128)}) while((s32[]{:T(128)}, f32[4,32,3,128]{3,2,1,0:T(4,128)S(1)}, f32[4,32,3,128]{3,2,1,0:T(4,128)S(1)}, s32[4,32,128]{2,1,0:T(8,128)S(1)}, ...), condition=%wide.region_12.13_spmd, body=%wide.region_11.12_spmd.sunk | while | flops 24653824 | bytes 623701 | solution.py:120
  426.5 10.2 fusion.182
  436.7 10.2 fusion.182
  447.0 10.2 fusion.182
  457.3 10.2 fusion.182
  468.5 13.0 all_gather.6
  487.2 13.0 scatter_fusion.1
  501.6 35.6 %while.57 = (s32[]{:T(128)}, f32[4,32,3,128]{3,2,1,0:T(4,128)S(1)}, f32[4,32,3,128]{3,2,1,0:T(4,128)S(1)}, s32[4,32,128]{2,1,0:T(8,128)S(1)}, f32[4,32,4,128]{3,1,2,0:T(8,128)S(1)}, /*index=5*/s32[]{:T(128)}) while((s32[]{:T(128)}, f32[4,32,3,128]{3,2,1,0:T(4,128)S(1)}, f32[4,32,3,128]{3,2,1,0:T(4,128)S(1)}, s32[4,32,128]{2,1,0:T(8,128)S(1)}, ...), condition=%wide.region_18.19_spmd, body=%wide.region_17.18_spmd.sunk | while | flops 24653824 | bytes 623701 | solution.py:87
  501.7 8.8 fusion.185
  510.6 8.8 fusion.185
  519.5 8.8 fusion.185
  528.4 8.8 fusion.185
  537.2 4.9 copy.50
  542.1 89.1 %scatter_custom_fusion.3 = f32[3,4224]{0,1:T(8,128)} fusion(s32[16384]{0:T(1024)} %copy-done.11, f32[16384,3]{1,0:T(8,128)} %bitcast.184, f32[]{:T(128)} %constant.206.clone.1), kind=kCustom, calls=%fused_computation.203 | custom fusion | flops 49152 | bytes 51200 | tf_op jit(solution)/shard_map/scatter-add | solution.py:92
  639.5 77.2 %psum.51 = f32[3,4096]{0,1:T(8,128)} all-reduce(f32[3,4096]{0,1:T(8,128)} %fusion.156), channel_id=1, replica_groups=mesh['src'=4,'tm'=8] {'src'}, use_global_device_ids=true, to_apply=%region_20.21 | all-reduce | flops 12288 | bytes 98304 | tf_op jit(solution)/shard_map/psum | solution.py:95
  716.6 4.1 multiply_reduce_fusion.1
  725.1 38.9 %all-reduce.1 = (f32[]{:T(128)}, f32[]{:T(128)}) all-reduce(f32[]{:T(128)S(6)} %add.363, f32[]{:T(128)S(6)} %add.370), channel_id=1, replica_groups=mesh['src'=4,'tm'=8] {'src','tm'}, use_global_device_ids=true, to_apply=%region_9.10 | all-reduce | flops 2 | bytes 16 | tf_op jit(solution)/shard_map/psum | solution.py:101
  769.7 41.1 %psum.53 = f32[]{:T(128)} all-reduce(f32[]{:T(128)S(6)} %add.373), channel_id=1, replica_groups=mesh['src'=4,'tm'=8] {'src','tm'}, use_global_device_ids=true, to_apply=%region_25.26 | all-reduce | flops 1 | bytes 8 | tf_op jit(solution)/shard_map/psum | solution.py:101
  812.1 3.2 multiply_add_fusion.1
  815.4 11.1 all_gather.7
  836.6 168.5 %while.61 = (s32[]{:T(128)}, f32[3,4224]{1,0:T(4,128)S(1)}, s32[128,2]{0,1:T(2,128)S(1)}, f32[128,3,128]{2,1,0:T(4,128)S(1)}, s32[]{:T(128)}) while((s32[]{:T(128)}, f32[3,4224]{1,0:T(4,128)S(1)}, s32[128,2]{0,1:T(2,128)S(1)}, f32[128,3,128]{2,1,0:T(4,128)S(1)}, s32[]{:T(128)}) %tuple.219), condition=%wide.while_cond.4, body=%wide.while_body.4.sunk | while | flops 2 | bytes 4201 | solution.py:72
  1005.9 37.5 %while.58 = (s32[]{:T(128)}, f32[4,32,3,128]{3,2,1,0:T(4,128)S(1)}, f32[4,32,3,128]{3,2,1,0:T(4,128)}, s32[4,32,128]{2,1,0:T(8,128)S(1)}, f32[4,32,4,128]{3,1,2,0:T(8,128)S(1)}, /*index=5*/s32[]{:T(128)}) while((s32[]{:T(128)}, f32[4,32,3,128]{3,2,1,0:T(4,128)S(1)}, f32[4,32,3,128]{3,2,1,0:T(4,128)}, s32[4,32,128]{2,1,0:T(8,128)S(1)}, ...), condition=%wide.region_28.29_spmd, body=%wide.region_27.28_spmd.sunk | while | flops 24653824 | bytes 623701 | solution.py:120
  1005.9 9.3 fusion.188
  1015.3 9.3 fusion.188
  1024.7 9.3 fusion.188
  1034.1 9.3 fusion.188
  1045.3 9.5 scatter_fusion.2
  1057.0 38.0 %while.59 = (s32[]{:T(128)}, f32[4,32,3,128]{3,2,1,0:T(4,128)S(1)}, f32[4,32,3,128]{3,2,1,0:T(4,128)S(1)}, s32[4,32,128]{2,1,0:T(8,128)}, f32[4,32,4,128]{3,1,2,0:T(8,128)S(1)}, /*index=5*/s32[]{:T(128)}) while((s32[]{:T(128)}, f32[4,32,3,128]{3,2,1,0:T(4,128)S(1)}, f32[4,32,3,128]{3,2,1,0:T(4,128)S(1)}, s32[4,32,128]{2,1,0:T(8,128)}, ...), condition=%wide.region_34.35_spmd, body=%wide.region_33.34_spmd.sunk | while | flops 24653824 | bytes 623701 | solution.py:87
  1057.8 8.7 fusion.191
  1067.3 8.7 fusion.191
  1076.8 8.7 fusion.191
  1086.3 8.7 fusion.191
  1095.0 4.9 copy.59
  1099.9 89.1 %scatter_custom_fusion.5 = f32[3,4224]{0,1:T(8,128)} fusion(s32[16384]{0:T(1024)} %copy-done.11, f32[16384,3]{1,0:T(8,128)} %bitcast.182, f32[]{:T(128)} %constant.206.clone.1), kind=kCustom, calls=%fused_computation.201 | custom fusion | flops 49152 | bytes 51200 | tf_op jit(solution)/shard_map/scatter-add | solution.py:92
  1198.0 78.3 %psum.54 = f32[3,4096]{0,1:T(8,128)} all-reduce(f32[3,4096]{0,1:T(8,128)} %fusion.157), channel_id=1, replica_groups=mesh['src'=4,'tm'=8] {'src'}, use_global_device_ids=true, to_apply=%region_36.37 | all-reduce | flops 12288 | bytes 98304 | tf_op jit(solution)/shard_map/psum | solution.py:95
  1276.3 3.4 fusion.135
  1282.6 38.5 %psum.55 = f32[]{:T(128)} all-reduce(f32[]{:T(128)S(6)} %add.380), channel_id=1, replica_groups=mesh['src'=4,'tm'=8] {'src','tm'}, use_global_device_ids=true, to_apply=%region_38.39 | all-reduce | flops 1 | bytes 8 | tf_op jit(solution)/shard_map/psum | solution.py:128
  1322.4 3.1 multiply_add_fusion
  (967 shorter events, 426.5 us)
Async XLA Ops:
  7.2 460.3 %reduce-scatter.4.cloned.1.call-start = ((), (), s32[]{:S(2)}) async-start(), calls=%async_computation.3 | async-start | bytes 1179648 | tf_op jit(solution)/shard_map/reduce_scatter | solution.py:69
  12.5 6.3 copy-start.13
  12.5 6.4 copy-start.3
  12.7 6.4 copy-start.10
  12.8 6.4 copy-start.5
  17.7 1.0 copy-start.2
  18.8 703.4 %reduce-scatter.6.cloned.1.call-start = ((), (), s32[]{:S(2)}) async-start(), calls=%async_computation.4 | async-start | bytes 1179648 | tf_op jit(solution)/shard_map/reduce_scatter | solution.py:69
  18.9 40.8 %copy-start.11 = (s32[16384]{0:T(1024)}, s32[16384]{0:T(1024)S(1)}, u32[]{:S(2)}) copy-start(s32[16384]{0:T(1024)S(1)} %fusion.158) | copy-start | bytes 196612
  149.7 6.1 collective-permute-start
  238.0 3.1 collective-permute-start.1
  467.4 17.3 %copy-start = (f32[128,5,128]{2,0,1:T(8,128)S(1)}, f32[128,5,128]{2,0,1:T(8,128)}, u32[]{:S(2)}) copy-start(f32[128,5,128]{2,0,1:T(8,128)} %param.25) | copy-start | bytes 983044
  468.5 16.6 %copy-start.12 = (s32[128]{0:T(128)S(1)}, s32[128]{0:T(128)}, u32[]{:S(2)}) copy-start(s32[128]{0:T(128)} %param.32) | copy-start | bytes 1540
  500.3 780.1 %reduce-scatter.8.cloned.1.call-start = ((), (), s32[]{:S(2)}) async-start(), calls=%async_computation.5 | async-start | bytes 1179648 | tf_op jit(solution)/shard_map/reduce_scatter | solution.py:69
  632.0 5.3 collective-permute-start.2
  716.6 5.5 copy-start.4
  815.3 18.9 %copy-start.7 = (f32[32,5,128]{2,1,0:T(8,128)}, f32[32,5,128]{2,1,0:T(8,128)S(1)}, u32[]{:S(2)}) copy-start(f32[32,5,128]{2,1,0:T(8,128)S(1)} %multiply_add_fusion.4) | copy-start | bytes 245764
  831.3 5.1 collective-permute-start.3
  1005.1 0.7 copy-start.9
  1043.4 0.9 copy-start.6
  1054.8 1.0 copy-start.1
  1189.8 6.1 collective-permute-start.4
  1276.3 4.1 copy-start.8
Sparse Core Ops, SparseCore 0:
  18.9 39.0 reduce-scatter.3
  500.4 34.3 reduce-scatter.5
  1056.0 36.2 reduce-scatter.7
where the time goes:
time: 1340 us
  local copies, waits for them, and re-layouts  405 us (30%)
  blocking collectives  378 us (28%)
  other arithmetic  332 us (25%)
  matrix products  183 us (14%)
  between operations  23.2 us (2%)
    gather x768, local copies, waits for them, and re-layouts  353 us
    scatter-add x3, other arithmetic, adjoint(): jnp.zeros((3, KN + HW), jnp.float32).at[:, window_index].add(win_sums)  267 us
    psum x3, blocking collectives, adjoint(): return (src_term, lax.psum(own_part, 'src'))  235 us
    dot_general x12, matrix products, adjoint_block(): jnp.einsum('trk,tar->tak', basis, scaled, precision=lax.Precision.HIGHEST)  106 us
    psum x2, blocking collectives, norm_sum(): return lax.psum(local_dot(vector, vector), ('src', 'tm'))  80 us
    dot_general x8, matrix products, forward_block(): jnp.einsum('trk,tak->tar', basis, window, precision=lax.Precision.HIGHEST)  77.9 us
    psum x1, blocking collectives, shards(): curv = lax.psum(local_dot(direction, image), ('src', 'tm'))  38.5 us
    scatter-add x3, other arithmetic, return_sources(): jax.ops.segment_sum(src_part, shard_block, num_segments=tm_count * SB_DEV)  27.4 us
  transfers between devices with their start and end apart: 8, of which 1 were waited for; matrix products, arithmetic and copies ran while one was open for 49% of the time, Pallas kernels for 0%

commit v1 on v0

--- a/solution.py
+++ b/solution.py
@@ -8,6 +8,24 @@
 SB_DEV = 32
 ITERS = 2
 damping = 1.0
+
+
+def joined_along(pieces, dim):
+    pieces = jnp.moveaxis(pieces, 0, dim)
+    dims = pieces.shape
+    return pieces.reshape(*dims[:dim], dims[dim] * dims[dim + 1], *dims[dim + 2 :])
+
+
+def collected_by_bits(value, axis):
+    size = lax.axis_size(axis)
+    pieces = value[None]
+    for level in range(size.bit_length() - 1):
+        bit = 1 << level
+        received = lax.ppermute(pieces, axis, [(i, i ^ bit) for i in range(size)])
+        both = jnp.stack([pieces, received])
+        upper = lax.axis_index(axis) >> level & 1
+        pieces = jnp.where(upper == 0, both, both[::-1]).reshape(-1, *value.shape)
+    return pieces
 
 
 def passed_along(block, axis, distance):
@@ -112,7 +130,7 @@
     norm_now = norm_sum(residual)
     for step in range(ITERS):
         dir_att = direction[1]
-        whole = lax.all_gather(direction[0], "tm", axis=0, tiled=True)
+        whole = joined_along(collected_by_bits(direction[0], "tm"), 0)
         src_tiles = whole[shard_block]
         rim_knots = passed_along(dir_att[:, :HW], "tm", -1)
         forward_extended = jnp.concatenate([dir_att, rim_knots], axis=1)

time: 1340 us -> 1490 us (1.11)
  local copies, waits for them, and re-layouts: 405 us -> 560 us
  blocking collectives: 378 us -> 353 us
    gather x768, local copies, waits for them, and re-layouts: 353 us -> 506 us
    all_gather x2 -> x0, blocking collectives: 24 us -> none  [shards(): whole = lax.all_gather(direction[0], 'tm', axis=0, tiled=True)]
  transfers between devices with their start and end apart: 8 -> 14, of which waited for: 1 -> 3; matrix products, arithmetic and copies ran while one was open for 49% -> 68% of each run, Pallas kernels for 0% -> 0%
where the time goes in v1:
time: 1490 us; the launch traced here: 1480 us
  local copies, waits for them, and re-layouts  560 us (38%)
  blocking collectives  353 us (24%)
  other arithmetic  342 us (23%)
  matrix products  178 us (12%)
  between operations  23.3 us (2%)
  starting transfers between devices  20.1 us (1%)
    gather x768, local copies, waits for them, and re-layouts  506 us
    scatter-add x3, other arithmetic, adjoint(): jnp.zeros((3, KN + HW), jnp.float32).at[:, window_index].add(win_sums)  267 us
    psum x3, blocking collectives, adjoint(): return (src_term, lax.psum(own_part, 'src'))  237 us
    dot_general x12, matrix products, adjoint_block(): jnp.einsum('trk,tar->tak', basis, scaled, precision=lax.Precision.HIGHEST)  102 us
    psum x2, blocking collectives, norm_sum(): return lax.psum(local_dot(vector, vector), ('src', 'tm'))  78.2 us
    dot_general x8, matrix products, forward_block(): jnp.einsum('trk,tak->tar', basis, window, precision=lax.Precision.HIGHEST)  76.5 us
    psum x1, blocking collectives, shards(): curv = lax.psum(local_dot(direction, image), ('src', 'tm'))  38.2 us
  transfers between devices with their start and end apart: 14, of which 3 were waited for; matrix products, arithmetic and copies ran while one was open for 68% of the time, Pallas kernels for 0%

profile of v1, /device:TPU:0, one launch (start us, length us, event | category | flops | bytes accessed | tf_op | source)
XLA Modules:
  0.0 1479.9 jit_solution(13162129571761142958)
XLA Ops:
  12.8 4.9 scatter_fusion
  19.1 35.6 %while.55 = (s32[]{:T(128)}, f32[4,32,3,128]{3,2,1,0:T(4,128)S(1)}, f32[4,32,3,128]{3,2,1,0:T(4,128)S(1)}, s32[4,32,128]{2,1,0:T(8,128)S(1)}, f32[4,32,4,128]{3,1,2,0:T(8,128)S(1)}, /*index=5*/s32[]{:T(128)}) while((s32[]{:T(128)}, f32[4,32,3,128]{3,2,1,0:T(4,128)S(1)}, f32[4,32,3,128]{3,2,1,0:T(4,128)S(1)}, s32[4,32,128]{2,1,0:T(8,128)S(1)}, ...), condition=%wide.region_4.5_spmd, body=%wide.region_3.4_spmd.sunk | while | flops 24653824 | bytes 623701 | solution.py:105
  19.2 8.8 fusion.183
  28.1 8.8 fusion.183
  37.0 8.8 fusion.183
  45.9 8.8 fusion.183
  54.7 4.9 copy.49
  59.7 89.1 %scatter_custom_fusion.1 = f32[3,4224]{0,1:T(8,128)} fusion(s32[16384]{0:T(1024)S(1)} %fusion.162, f32[16384,3]{1,0:T(8,128)} %bitcast.212, f32[]{:T(128)} %constant.210.clone.1), kind=kCustom, calls=%fused_computation.205 | custom fusion | flops 49152 | bytes 51200 | tf_op jit(solution)/shard_map/scatter-add | solution.py:110
  152.1 3.1 slice.203
  157.9 80.0 %psum.49 = f32[3,4096]{0,1:T(8,128)S(1)} all-reduce(f32[3,4096]{0,1:T(8,128)} %fusion.159), channel_id=1, replica_groups=mesh['src'=4,'tm'=8] {'src'}, use_global_device_ids=true, to_apply=%region_7.8 | all-reduce | flops 12288 | bytes 98304 | tf_op jit(solution)/shard_map/psum | solution.py:113
  248.9 260.4 %while.60 = (s32[]{:T(128)}, f32[3,4224]{1,0:T(4,128)}, s32[128,2]{0,1:T(2,128)S(1)}, f32[128,3,128]{2,1,0:T(4,128)S(1)}, s32[]{:T(128)}) while((s32[]{:T(128)}, f32[3,4224]{1,0:T(4,128)}, s32[128,2]{0,1:T(2,128)S(1)}, f32[128,3,128]{2,1,0:T(4,128)S(1)}, s32[]{:T(128)}) %tuple.183), condition=%wide.while_cond.3, body=%wide.while_body.3.sunk | while | flops 2 | bytes 3689 | solution.py:90
  510.3 37.5 %while.56 = (s32[]{:T(128)}, f32[4,32,3,128]{3,2,1,0:T(4,128)S(1)}, f32[4,32,3,128]{3,2,1,0:T(4,128)}, s32[4,32,128]{2,1,0:T(8,128)S(1)}, f32[4,32,4,128]{3,1,2,0:T(8,128)S(1)}, /*index=5*/s32[]{:T(128)}) while((s32[]{:T(128)}, f32[4,32,3,128]{3,2,1,0:T(4,128)S(1)}, f32[4,32,3,128]{3,2,1,0:T(4,128)}, s32[4,32,128]{2,1,0:T(8,128)S(1)}, ...), condition=%wide.region_12.13_spmd, body=%wide.region_11.12_spmd.sunk | while | flops 24653824 | bytes 623701 | solution.py:138
  510.3 9.3 fusion.186
  519.7 9.3 fusion.186
  529.1 9.3 fusion.186
  538.5 9.3 fusion.186
  554.8 13.0 scatter_fusion.1
  569.9 32.1 %while.57 = (s32[]{:T(128)}, f32[4,32,3,128]{3,2,1,0:T(4,128)S(1)}, f32[4,32,3,128]{3,2,1,0:T(4,128)}, s32[4,32,128]{2,1,0:T(8,128)S(1)}, f32[4,32,4,128]{3,1,2,0:T(8,128)S(1)}, /*index=5*/s32[]{:T(128)}) while((s32[]{:T(128)}, f32[4,32,3,128]{3,2,1,0:T(4,128)S(1)}, f32[4,32,3,128]{3,2,1,0:T(4,128)}, s32[4,32,128]{2,1,0:T(8,128)S(1)}, ...), condition=%wide.region_18.19_spmd, body=%wide.region_17.18_spmd.sunk | while | flops 24653824 | bytes 623701 | solution.py:105
  570.0 7.9 fusion.189
  578.0 7.9 fusion.189
  586.0 8.0 fusion.189
  594.1 7.9 fusion.189
  602.0 4.9 copy.59
  606.9 89.1 %scatter_custom_fusion.3 = f32[3,4224]{0,1:T(8,128)} fusion(s32[16384]{0:T(1024)} %copy-done.14, f32[16384,3]{1,0:T(8,128)} %bitcast.214, f32[]{:T(128)} %constant.210.clone.1), kind=kCustom, calls=%fused_computation.203 | custom fusion | flops 49152 | bytes 51200 | tf_op jit(solution)/shard_map/scatter-add | solution.py:110
  698.8 3.1 slice.207
  704.0 78.0 %psum.51 = f32[3,4096]{0,1:T(8,128)} all-reduce(f32[3,4096]{0,1:T(8,128)} %fusion.160), channel_id=1, replica_groups=mesh['src'=4,'tm'=8] {'src'}, use_global_device_ids=true, to_apply=%region_20.21 | all-reduce | flops 12288 | bytes 98304 | tf_op jit(solution)/shard_map/psum | solution.py:113
  782.0 4.1 multiply_reduce_fusion.1
  790.4 38.5 %all-reduce.1 = (f32[]{:T(128)}, f32[]{:T(128)}) all-reduce(f32[]{:T(128)S(6)} %add.363, f32[]{:T(128)S(6)} %add.370), channel_id=1, replica_groups=mesh['src'=4,'tm'=8] {'src','tm'}, use_global_device_ids=true, to_apply=%region_9.10 | all-reduce | flops 2 | bytes 16 | tf_op jit(solution)/shard_map/psum | solution.py:119
  834.7 39.7 %psum.53 = f32[]{:T(128)} all-reduce(f32[]{:T(128)S(6)} %add.373), channel_id=1, replica_groups=mesh['src'=4,'tm'=8] {'src','tm'}, use_global_device_ids=true, to_apply=%region_25.26 | all-reduce | flops 1 | bytes 8 | tf_op jit(solution)/shard_map/psum | solution.py:119
  887.9 245.9 %while.61 = (s32[]{:T(128)}, f32[3,4224]{1,0:T(4,128)}, s32[128,2]{0,1:T(2,128)S(1)}, f32[128,3,128]{2,1,0:T(4,128)S(1)}, s32[]{:T(128)}) while((s32[]{:T(128)}, f32[3,4224]{1,0:T(4,128)}, s32[128,2]{0,1:T(2,128)S(1)}, f32[128,3,128]{2,1,0:T(4,128)S(1)}, s32[]{:T(128)}) %tuple.221), condition=%wide.while_cond.4, body=%wide.while_body.4.sunk | while | flops 2 | bytes 3689 | solution.py:90
  1139.2 42.4 %while.58 = (s32[]{:T(128)}, f32[4,32,3,128]{3,2,1,0:T(4,128)}, f32[4,32,3,128]{3,2,1,0:T(4,128)}, s32[4,32,128]{2,1,0:T(8,128)}, f32[4,32,4,128]{3,1,2,0:T(8,128)S(1)}, /*index=5*/s32[]{:T(128)}) while((s32[]{:T(128)}, f32[4,32,3,128]{3,2,1,0:T(4,128)}, f32[4,32,3,128]{3,2,1,0:T(4,128)}, s32[4,32,128]{2,1,0:T(8,128)}, ...), condition=%wide.region_28.29_spmd, body=%wide.region_27.28_spmd.sunk | while | flops 24653824 | bytes 623701 | solution.py:138
  1140.0 9.8 fusion.192
  1150.6 9.8 fusion.192
  1161.2 9.8 fusion.192
  1171.8 9.8 fusion.192
  1190.8 9.5 scatter_fusion.2
  1202.4 38.0 %while.59 = (s32[]{:T(128)}, f32[4,32,3,128]{3,2,1,0:T(4,128)S(1)}, f32[4,32,3,128]{3,2,1,0:T(4,128)S(1)}, s32[4,32,128]{2,1,0:T(8,128)}, f32[4,32,4,128]{3,1,2,0:T(8,128)S(1)}, /*index=5*/s32[]{:T(128)}) while((s32[]{:T(128)}, f32[4,32,3,128]{3,2,1,0:T(4,128)S(1)}, f32[4,32,3,128]{3,2,1,0:T(4,128)S(1)}, s32[4,32,128]{2,1,0:T(8,128)}, ...), condition=%wide.region_34.35_spmd, body=%wide.region_33.34_spmd.sunk | while | flops 24653824 | bytes 623701 | solution.py:105
  1203.2 8.7 fusion.195
  1212.7 8.7 fusion.195
  1222.2 8.7 fusion.195
  1231.7 8.7 fusion.195
  1240.4 4.9 copy.70
  1245.3 89.1 %scatter_custom_fusion.5 = f32[3,4224]{0,1:T(8,128)} fusion(s32[16384]{0:T(1024)} %copy-done.14, f32[16384,3]{1,0:T(8,128)} %bitcast.213, f32[]{:T(128)} %constant.210.clone.1), kind=kCustom, calls=%fused_computation.201 | custom fusion | flops 49152 | bytes 51200 | tf_op jit(solution)/shard_map/scatter-add | solution.py:110
  1337.0 3.1 slice.211
  1342.1 78.9 %psum.54 = f32[3,4096]{0,1:T(8,128)} all-reduce(f32[3,4096]{0,1:T(8,128)} %fusion.161), channel_id=1, replica_groups=mesh['src'=4,'tm'=8] {'src'}, use_global_device_ids=true, to_apply=%region_36.37 | all-reduce | flops 12288 | bytes 98304 | tf_op jit(solution)/shard_map/psum | solution.py:113
  1421.0 3.4 fusion.135
  1427.3 38.2 %psum.55 = f32[]{:T(128)} all-reduce(f32[]{:T(128)S(6)} %add.380), channel_id=1, replica_groups=mesh['src'=4,'tm'=8] {'src','tm'}, use_global_device_ids=true, to_apply=%region_38.39 | all-reduce | flops 1 | bytes 8 | tf_op jit(solution)/shard_map/psum | solution.py:146
  1466.7 3.2 multiply_add_fusion
  (997 shorter events, 594.5 us)
Async XLA Ops:
  7.2 234.1 %reduce-scatter.4.cloned.1.call-start = ((), (), s32[]{:S(2)}) async-start(), calls=%async_computation.3 | async-start | bytes 1179648 | tf_op jit(solution)/shard_map/reduce_scatter | solution.py:87
  12.5 6.3 copy-start.4
  12.7 6.3 copy-start.13
  12.8 6.3 copy-start.7
  17.7 1.0 copy-start.3
  18.7 768.7 %reduce-scatter.6.cloned.1.call-start = ((), (), s32[]{:S(2)}) async-start(), calls=%async_computation.4 | async-start | bytes 1179648 | tf_op jit(solution)/shard_map/reduce_scatter | solution.py:87
  54.7 4.9 copy-start.16
  59.7 95.4 %copy-start.14 = (s32[16384]{0:T(1024)}, s32[16384]{0:T(1024)S(1)}, u32[]{:S(2)}) copy-start(s32[16384]{0:T(1024)S(1)} %fusion.162) | copy-start | bytes 196612
  149.7 6.2 collective-permute-start
  238.0 3.1 collective-permute-start.4
  241.2 3.7 collective-permute-start.1
  245.9 263.4 %collective-permute-start.2 = (f32[2,32,5,128]{3,2,1,0:T(8,128)S(1)}, f32[2,32,5,128]{3,2,1,0:T(8,128)S(1)}, u32[]{:S(2)}, u32[]{:S(2)}) collective-permute-start(f32[2,32,5,128]{3,2,1,0:T(8,128)S(1)} %get-tuple-element.335), channel_id=1, source_target_pairs={{0,2},{1,3},{2,0},{3,1},{4,6},{5,7},{6,4},{7,5},{8,10},{9,11},{10,... | collective-permute-start | bytes 491528 | tf_op jit(solution)/shard_map/ppermute | solution.py:24
  509.3 0.9 copy-start.11
  510.2 37.7 %collective-permute-start.3 = (f32[4,32,5,128]{3,1,0,2:T(8,128)}, f32[4,32,5,128]{3,1,0,2:T(8,128)}, u32[]{:S(2)}, u32[]{:S(2)}) collective-permute-start(f32[4,32,5,128]{3,1,0,2:T(8,128)} %copy.50), channel_id=1, source_target_pairs={{0,4},{1,5},{2,6},{3,7},{4,0},{5,1},{6,2},{7,3},{8,12},{9,13},{10,... | collective-permute-start | bytes 983048 | tf_op jit(solution)/shard_map/ppermute | solution.py:24
  510.2 37.5 %copy-start.5 = (f32[128,3,128]{2,0,1:T(8,128)S(1)}, f32[128,3,128]{2,0,1:T(8,128)}, u32[]{:S(2)}) copy-start(f32[128,3,128]{2,0,1:T(8,128)} %param.26) | copy-start | bytes 589828
  548.9 3.4 copy-start.1
  549.0 3.7 copy-start.15
  567.9 857.2 %reduce-scatter.8.cloned.1.call-start = ((), (), s32[]{:S(2)}) async-start(), calls=%async_computation.5 | async-start | bytes 1179648 | tf_op jit(solution)/shard_map/reduce_scatter | solution.py:87
  602.0 4.9 copy-start.8
  696.8 5.0 collective-permute-start.5
  782.0 5.5 copy-start.6
  877.5 1.3 copy-start
  878.8 5.0 collective-permute-start.9
  880.3 253.5 %copy-start.9 = (f32[32,5,128]{2,1,0:T(8,128)}, f32[32,5,128]{2,1,0:T(8,128)S(1)}, u32[]{:S(2)}) copy-start(f32[32,5,128]{2,1,0:T(8,128)S(1)} %multiply_add_fusion.4) | copy-start | bytes 245764
  882.6 2.1 collective-permute-start.6
  885.6 248.2 %collective-permute-start.7 = (f32[2,32,5,128]{3,2,1,0:T(8,128)}, f32[2,32,5,128]{3,2,1,0:T(8,128)}, u32[]{:S(2)}, u32[]{:S(2)}) collective-permute-start(f32[2,32,5,128]{3,2,1,0:T(8,128)} %get-tuple-element.333), channel_id=1, source_target_pairs={{0,2},{1,3},{2,0},{3,1},{4,6},{5,7},{6,4},{7,5},{8,10},{9,11},{10,... | collective-permute-start | bytes 491528 | tf_op jit(solution)/shard_map/ppermute | solution.py:24
  1133.8 0.7 copy-start.12
  1136.4 46.8 %collective-permute-start.8 = (f32[4,32,5,128]{3,1,0,2:T(8,128)}, f32[4,32,5,128]{3,1,0,2:T(8,128)}, u32[]{:S(2)}, u32[]{:S(2)}) collective-permute-start(f32[4,32,5,128]{3,1,0,2:T(8,128)} %copy.61), channel_id=1, source_target_pairs={{0,4},{1,5},{2,6},{3,7},{4,0},{5,1},{6,2},{7,3},{8,12},{9,13},{10,... | collective-permute-start | bytes 983048 | tf_op jit(solution)/shard_map/ppermute | solution.py:24
  1200.2 1.0 copy-start.2
  1335.3 4.8 collective-permute-start.10
  1421.0 4.1 copy-start.10
Sparse Core Ops, SparseCore 0:
  18.9 39.0 reduce-scatter.3
  568.0 34.5 reduce-scatter.5
  1201.4 33.8 reduce-scatter.7
